TPU v7x, 32 devices: a whole 2x2x4 slice. The times are simulated.
32 devices in a mesh: dp: 4 (over x, core), expert: 8 (over z, y).
Axes of the slice: x: 2, y: 2, z: 4, core: 2. Of those that a mesh axis runs over, the one named last changes fastest.
Arguments:
- tokens: bfloat16 [4096, 2048], P(('dp', 'expert')), may hold values from -6 to 6
- out_grad: bfloat16 [4096, 2048], P(('dp', 'expert')), may hold values from -6 to 6
- w_in: bfloat16 [2048, 512], replicated, may hold values from -0.125 to 0.125
- w_out: bfloat16 [512, 2048], replicated, may hold values from -0.25 to 0.25
- w_gate: bfloat16 [8, 512, 1024], P('expert'), may hold values from -0.25 to 0.25
- w_up: bfloat16 [8, 512, 1024], P('expert'), may hold values from -0.25 to 0.25
- w_down: bfloat16 [8, 1024, 512], P('expert'), may hold values from -0.1875 to 0.1875
- gate_logits: float32 [4096, 2], P(('dp', 'expert')), may hold values from -8 to 8
- expert_ids: int32 [4096, 2], P(('dp', 'expert')), may hold values from 0 to 7, all different within a row; in each aligned block of 128 rows (0 to 127, 128 to 255, ...) at most 48 rows name the same one
Outputs:
- token_grad: bfloat16 [4096, 2048], P(('dp', 'expert'))
- logit_grad: float32 [4096, 2], P(('dp', 'expert'))
- grad_in: float32 [8, 2048, 512], P('expert', 'dp')
- grad_out: float32 [8, 512, 2048], P('expert', None, 'dp')
Inputs may be any that keep to these rules, and one draw needn't show every extreme that they name: `expert_ids`: each row names 2 different experts. Among the 128 rows of one device (aligned blocks) no expert is named more than 48 times, a bound that some block reaches.
All inputs are finite; a program needn't handle non-finite values.
Results may differ from a plain program's by a relative error of at most 0.01.
Values may be sent and summed in bfloat16 or wider, within the bound.
A program may use at most 64 MiB of HBM per device.

v0:
```python
import jax
import jax.numpy as jnp
from jax import lax
from jax.sharding import PartitionSpec as P


def forward_rows(z_rows, w_gate, w_up, w_down):
    pre_a = jnp.einsum("sxnl,xlh->sxnh", z_rows, w_gate, preferred_element_type=jnp.float32)
    pre_b = jnp.einsum("sxnl,xlh->sxnh", z_rows, w_up, preferred_element_type=jnp.float32)
    sig = jax.nn.sigmoid(pre_a)
    hidden = (pre_a * sig * pre_b).astype(jnp.bfloat16)
    outv = jnp.einsum("sxnh,xhl->sxnl", hidden, w_down, preferred_element_type=jnp.float32).astype(
        jnp.bfloat16
    )
    return (outv, pre_a, pre_b, sig)


def backward_rows(g_rows, pre_a, pre_b, sig, w_gate, w_up, w_down):
    hid_grad = jnp.einsum("sxnl,xhl->sxnh", g_rows, w_down, preferred_element_type=jnp.float32)
    grad_a = (hid_grad * pre_b * sig * (1.0 + pre_a * (1.0 - sig))).astype(jnp.bfloat16)
    grad_b = (hid_grad * pre_a * sig).astype(jnp.bfloat16)
    grad_z = jnp.einsum("sxnh,xlh->sxnl", grad_a, w_gate, preferred_element_type=jnp.float32)
    grad_z = grad_z + jnp.einsum("sxnh,xlh->sxnl", grad_b, w_up, preferred_element_type=jnp.float32)
    return grad_z.astype(jnp.bfloat16)


def body(tokens, out_grad, w_in, w_out, w_gate, w_up, w_down, gate_logits, expert_ids):
    tok_rows, top = expert_ids.shape
    groups = lax.axis_size("expert")
    experts_here = w_gate.shape[0]
    experts = groups * experts_here
    width_lat = w_in.shape[1]
    capacity = 3 * tok_rows * top // (2 * experts)
    latent = jnp.dot(tokens, w_in, preferred_element_type=jnp.float32).astype(jnp.bfloat16)
    lat_grad = lax.dot_general(
        out_grad, w_out, (((1,), (1,)), ((), ())), preferred_element_type=jnp.float32
    ).astype(jnp.bfloat16)
    score = jax.nn.sigmoid(gate_logits)
    total = jnp.sum(score, axis=1, keepdims=True)
    gate = score / total
    flat_ids = expert_ids.reshape(-1)
    onehot = (flat_ids[:, None] == jnp.arange(experts, dtype=jnp.int32)[None, :]).astype(jnp.int32)
    rank = jnp.cumsum(onehot, axis=0) - onehot
    slot = jnp.sum(rank * onehot, axis=1)
    position = flat_ids * capacity + slot
    source = jnp.arange(tok_rows * top, dtype=jnp.int32) // top
    z_send = (
        jnp.zeros((experts * capacity, width_lat), jnp.bfloat16).at[position].set(latent[source])
    )
    g_send = (
        jnp.zeros((experts * capacity, width_lat), jnp.bfloat16).at[position].set(lat_grad[source])
    )
    z_send = z_send.reshape(groups, experts_here, capacity, width_lat)
    g_send = g_send.reshape(groups, experts_here, capacity, width_lat)
    z_recv = lax.all_to_all(z_send, "expert", split_axis=0, concat_axis=0, tiled=True)
    outv, pre_a, pre_b, sig = forward_rows(z_recv, w_gate, w_up, w_down)
    back_out = lax.all_to_all(outv, "expert", split_axis=0, concat_axis=0, tiled=True)
    g_recv = lax.all_to_all(g_send, "expert", split_axis=0, concat_axis=0, tiled=True)
    grad_z = backward_rows(g_recv, pre_a, pre_b, sig, w_gate, w_up, w_down)
    back_grad = lax.all_to_all(grad_z, "expert", split_axis=0, concat_axis=0, tiled=True)
    back_out = back_out.reshape(experts * capacity, width_lat)
    back_grad = back_grad.reshape(experts * capacity, width_lat)
    expert_out = back_out[position].reshape(tok_rows, top, width_lat).astype(jnp.float32)
    choice_grad = back_grad[position].reshape(tok_rows, top, width_lat).astype(jnp.float32)
    mixed = jnp.sum(gate[:, :, None] * expert_out, axis=1).astype(jnp.bfloat16)
    gate_grad = jnp.sum(expert_out * lat_grad.astype(jnp.float32)[:, None, :], axis=2)
    centred = gate_grad - jnp.sum(gate * gate_grad, axis=1, keepdims=True)
    logit_grad = score * (1.0 - score) * centred / total
    latent_grad = jnp.sum(gate[:, :, None] * choice_grad, axis=1).astype(jnp.bfloat16)
    token_grad = lax.dot_general(
        latent_grad, w_in, (((1,), (1,)), ((), ())), preferred_element_type=jnp.float32
    ).astype(jnp.bfloat16)
    paired_left = jnp.stack([tokens, out_grad], axis=0)
    paired_right = jnp.stack([latent_grad, mixed], axis=0)
    shares = lax.psum_scatter(
        jnp.einsum(
            "btc,btl->cbl", paired_left, paired_right, preferred_element_type=jnp.float32
        ).astype(jnp.bfloat16),
        "dp",
        scatter_dimension=0,
        tiled=True,
    ).astype(jnp.float32)
    grad_in = shares[:, 0, :][None]
    grad_out = shares[:, 1, :].T[None]
    return (token_grad, logit_grad, grad_in, grad_out)


def solution(mesh):
    placed = (
        P(("dp", "expert"), None),
        P(("dp", "expert"), None),
        P(),
        P(),
        P("expert", None, None),
        P("expert", None, None),
        P("expert", None, None),
        P(("dp", "expert"), None),
        P(("dp", "expert"), None),
    )
    return jax.shard_map(
        body,
        mesh=mesh,
        in_specs=placed,
        out_specs=(
            P(("dp", "expert"), None),
            P(("dp", "expert"), None),
            P("expert", "dp", None),
            P("expert", None, "dp"),
        ),
        check_vma=False,
    )
```

profile of v0, /device:TPU:0, one launch (start us, length us, event | category | flops | bytes accessed | tf_op | source)
XLA Modules:
  0.0 149.9 jit_solution(9703826630668049541)
XLA Ops:
  10.3 1.6 %convolution_convert_fusion.2 = bf16[128,512]{1,0:T(8,128)(2,1)S(1)} fusion(bf16[128,2048]{1,0:T(8,128)(2,1)} %param.9, bf16[2048,512]{1,0:T(8,128)(2,1)S(1)} %copy-done), kind=kOutput, calls=%fused_computation.29 | convolution fusion | flops 268500992 | bytes 2752512 | tf_op jit(solution)/shard_map/dot_general | solution.py:34
  11.9 3.4 %scatter_custom_fusion.1 = bf16[384,512]{1,0:T(8,128)(2,1)} fusion(s32[256]{0:T(256)S(1)} %bitcast.170, bf16[128,512]{1,0:T(8,128)(2,1)S(1)} %convolution_convert_fusion.2, s32[1024]{0:T(1024)S(1)} %pad_clamp_fusion.1, bf16[]{:T(256)} %constant.28.clone.1), kind=kCustom, calls=%fused_computation.58 | custom fusion | bytes 393218 | tf_op jit(solution)/shard_map/scatter | solution.py:48
  15.3 7.3 %all-to-all-start.1 = ((bf16[8,1,48,512]{3,2,1,0:T(8,128)(2,1)}), bf16[8,1,48,512]{3,2,1,0:T(8,128)(2,1)S(1)}, u32[]{:S(2)}, u32[]{:S(2)}) async-start(bf16[8,1,48,512]{3,2,1,0:T(8,128)(2,1)} %bitcast.12), calls=%async_computation.1 | async-start | bytes 786432 | tf_op jit(solution)/shard_map/all_to_all | solution.py:55
  22.6 3.1 %fusion.55 = (f32[128,512]{1,0:T(8,128)}, bf16[128,512]{1,0:T(8,128)(2,1)S(1)}) fusion(bf16[128,2048]{1,0:T(8,128)(2,1)S(1)} %copy-done.1, bf16[512,2048]{1,0:T(8,128)(2,1)} %param.12), kind=kOutput, calls=%fused_computation.95 | convolution fusion | flops 268566528 | bytes 3014656 | tf_op jit(solution)/shard_map/dot_general | solution.py:35
  25.7 3.4 %scatter_custom_fusion = bf16[384,512]{1,0:T(8,128)(2,1)} fusion(s32[256]{0:T(256)S(1)} %bitcast.171, bf16[128,512]{1,0:T(8,128)(2,1)S(1)} %get-tuple-element.28, s32[1024]{0:T(1024)S(1)} %pad_clamp_fusion.1, bf16[]{:T(256)} %constant.28.clone.1), kind=kCustom, calls=%fused_computation.60 | custom fusion | bytes 393218 | tf_op jit(solution)/shard_map/scatter | solution.py:51
  29.1 5.2 %all-to-all-done.1 = bf16[8,1,48,512]{3,2,1,0:T(8,128)(2,1)S(1)} async-done(((bf16[8,1,48,512]{3,2,1,0:T(8,128)(2,1)}), bf16[8,1,48,512]{3,2,1,0:T(8,128)(2,1)S(1)}, u32[]{:S(2)}, u32[]{:S(2)}) %all-to-all-start.1) | async-done | bytes 393248 | tf_op jit(solution)/shard_map/all_to_all | solution.py:55
  34.3 3.6 %all-to-all-start = ((bf16[8,1,48,512]{3,2,1,0:T(8,128)(2,1)}), bf16[8,1,48,512]{3,2,1,0:T(8,128)(2,1)S(1)}, u32[]{:S(2)}, u32[]{:S(2)}) async-start(bf16[8,1,48,512]{3,2,1,0:T(8,128)(2,1)} %bitcast.5), calls=%async_computation | async-start | bytes 786432 | tf_op jit(solution)/shard_map/all_to_all | solution.py:58
  37.9 3.0 %fusion.18 = f32[8,48,1024]{2,1,0:T(8,128)} fusion(bf16[1,512,1024]{2,1,0:T(8,128)(2,1)} %param.13, bf16[8,1,48,512]{3,2,1,0:T(8,128)(2,1)S(1)} %all-to-all-done.1), kind=kOutput, calls=%fused_computation.38 | convolution fusion | flops 402653184 | bytes 3014656 | tf_op jit(solution)/shard_map/sxnl,xlh->sxnh/dot_general | solution.py:8
  40.9 1.7 %fusion.21 = f32[8,48,1024]{2,1,0:T(8,128)} fusion(bf16[1,512,1024]{2,1,0:T(8,128)(2,1)S(1)} %copy-done.4, bf16[8,1,48,512]{3,2,1,0:T(8,128)(2,1)S(1)} %all-to-all-done.1), kind=kOutput, calls=%fused_computation.41 | convolution fusion | flops 402653184 | bytes 3014656 | tf_op jit(solution)/shard_map/sxnl,xlh->sxnh/dot_general | solution.py:9
  42.7 6.8 %all-to-all-done = bf16[8,1,48,512]{3,2,1,0:T(8,128)(2,1)S(1)} async-done(((bf16[8,1,48,512]{3,2,1,0:T(8,128)(2,1)}), bf16[8,1,48,512]{3,2,1,0:T(8,128)(2,1)S(1)}, u32[]{:S(2)}, u32[]{:S(2)}) %all-to-all-start) | async-done | bytes 393248 | tf_op jit(solution)/shard_map/all_to_all | solution.py:58
  49.5 2.0 %fusion.24 = f32[8,48,1024]{2,1,0:T(8,128)S(1)} fusion(bf16[1,1024,512]{2,1,0:T(8,128)(2,1)} %param.15, bf16[8,1,48,512]{3,2,1,0:T(8,128)(2,1)S(1)} %all-to-all-done), kind=kOutput, calls=%fused_computation.44 | convolution fusion | flops 402653184 | bytes 3014656 | tf_op jit(solution)/shard_map/sxnl,xhl->sxnh/dot_general | solution.py:19
  51.5 2.5 %fusion.16 = f32[8,48,512]{2,1,0:T(8,128)S(1)} fusion(bf16[1,512,1024]{2,1,0:T(8,128)(2,1)S(1)} %copy-done.3, f32[8,48,1024]{2,1,0:T(8,128)} %fusion.21, f32[8,48,1024]{2,1,0:T(8,128)S(1)} %fusion.24, f32[8,48,1024]{2,1,0:T(8,128)S(1)} %copy-done.2), kind=kOutput, calls=%fused_computation.36 | convolution fusion | flops 406585344 | bytes 6553600 | tf_op jit(solution)/shard_map/sxnh,xlh->sxnl/dot_general | solution.py:22
  55.4 3.6 %all-to-all-start.2 = ((bf16[8,1,48,512]{3,2,1,0:T(8,128)(2,1)}), bf16[8,1,48,512]{3,2,1,0:T(8,128)(2,1)S(1)}, u32[]{:S(2)}, u32[]{:S(2)}) async-start(bf16[8,1,48,512]{3,2,1,0:T(8,128)(2,1)} %fusion.12), calls=%async_computation.2 | async-start | bytes 786432 | tf_op jit(solution)/shard_map/all_to_all | solution.py:60
  59.0 3.2 %fusion.11 = bf16[8,1,48,512]{3,2,1,0:T(8,128)(2,1)} fusion(bf16[1,1024,512]{2,1,0:T(8,128)(2,1)S(1)} %copy-done.6, f32[8,48,1024]{2,1,0:T(8,128)} %fusion.21, f32[8,48,1024]{2,1,0:T(8,128)} %fusion.18), kind=kOutput, calls=%fused_computation.27 | convolution fusion | flops 405209088 | bytes 4587520 | tf_op jit(solution)/shard_map/sxnh,xhl->sxnl/dot_general | solution.py:12
  62.3 7.9 %all-to-all-done.2 = bf16[8,1,48,512]{3,2,1,0:T(8,128)(2,1)S(1)} async-done(((bf16[8,1,48,512]{3,2,1,0:T(8,128)(2,1)}), bf16[8,1,48,512]{3,2,1,0:T(8,128)(2,1)S(1)}, u32[]{:S(2)}, u32[]{:S(2)}) %all-to-all-start.2) | async-done | bytes 393248 | tf_op jit(solution)/shard_map/all_to_all | solution.py:60
  70.1 3.7 %all-to-all-start.3 = ((bf16[8,1,48,512]{3,2,1,0:T(8,128)(2,1)}), bf16[8,1,48,512]{3,2,1,0:T(8,128)(2,1)S(1)}, u32[]{:S(2)}, u32[]{:S(2)}) async-start(bf16[8,1,48,512]{3,2,1,0:T(8,128)(2,1)} %fusion.11), calls=%async_computation.3 | async-start | bytes 786432 | tf_op jit(solution)/shard_map/all_to_all | solution.py:57
  74.2 1.9 %gather_fusion = bf16[256,512]{1,0:T(8,128)(2,1)} fusion(bf16[384,512]{1,0:T(8,128)(2,1)S(1)} %bitcast.164, s32[1024]{0:T(1024)S(1)} %pad_clamp_fusion), kind=kCustom, calls=%fused_computation.2 | custom fusion | bytes 525312 | tf_op jit(solution)/shard_map/gather | solution.py:64
  77.4 7.6 %all-to-all-done.3 = bf16[8,1,48,512]{3,2,1,0:T(8,128)(2,1)S(1)} async-done(((bf16[8,1,48,512]{3,2,1,0:T(8,128)(2,1)}), bf16[8,1,48,512]{3,2,1,0:T(8,128)(2,1)S(1)}, u32[]{:S(2)}, u32[]{:S(2)}) %all-to-all-start.3) | async-done | bytes 393248 | tf_op jit(solution)/shard_map/all_to_all | solution.py:57
  84.9 1.9 %gather_fusion.1 = bf16[256,512]{1,0:T(8,128)(2,1)} fusion(bf16[384,512]{1,0:T(8,128)(2,1)S(1)} %bitcast.165, s32[1024]{0:T(1024)S(1)} %pad_clamp_fusion), kind=kCustom, calls=%fused_computation.3 | custom fusion | bytes 525312 | tf_op jit(solution)/shard_map/gather | solution.py:63
  88.1 2.6 %multiply_reduce_fusion = (bf16[128,512]{1,0:T(8,128)(2,1)S(1)}, f32[128,2]{1,0:T(8,128)S(1)}, bf16[128,512]{1,0:T(8,128)(2,1)S(1)}) fusion(f32[128,2,512]{2,1,0:T(2,128)S(1)} %reshape.196, f32[128,2]{1,0:T(8,128)S(1)} %copy.30, f32[128,512]{1,0:T(8,128)} %get-tuple-element.27, f32[128,2,512]{2,1,0:T(2,128)S(1)} %reshape.195), kind=kLoop, calls=%fused_computation.49 | loop fusion | flops 655104 | bytes 1574912 | tf_op jit(solution)/shard_map/reduce_sum | solution.py:65
  90.9 4.4 %convert_bitcast_fusion = bf16[2048,2,512]{0,2,1:T(8,128)(2,1)} fusion(bf16[1,128,2048]{2,1,0:T(8,128)(2,1)} %bitcast.167, bf16[1,128,2048]{2,1,0:T(8,128)(2,1)} %bitcast.166, bf16[1,128,512]{1,2,0:T(8,128)(2,1)S(1)} %bitcast.169, bf16[1,128,512]{1,2,0:T(8,128)(2,1)S(1)} %bitcast.168), kind=kOutput, calls=%fused_computation.6 | convolution fusion | flops 539623424 | bytes 5505024 | tf_op jit(solution)/shard_map/btc,btl->cbl/dot_general | solution.py:76
  96.0 1.6 %convolution_convert_fusion = bf16[128,2048]{1,0:T(8,128)(2,1)} fusion(bf16[2048,512]{1,0:T(8,128)(2,1)S(1)} %copy-done, bf16[128,512]{0,1:T(8,128)(2,1)S(1)} %copy.35), kind=kOutput, calls=%fused_computation.7 | convolution fusion | flops 268697600 | bytes 2752512 | tf_op jit(solution)/shard_map/dot_general | solution.py:70
  97.6 41.4 %reduce-scatter.2.cloned.1.call-done = bf16[512,2,512]{0,2,1:T(8,128)(2,1)} async-done(((bf16[2048,2,512]{0,2,1:T(8,128)(2,1)}), bf16[512,2,512]{0,2,1:T(8,128)(2,1)}) %reduce-scatter.2.cloned.1.call-update) | async-done | bytes 1048592 | tf_op jit(solution)/shard_map/reduce_scatter | solution.py:75
  139.1 1.5 convert_element_type.130
  (47 shorter events, 10.9 us)
Async XLA Ops:
  7.2 3.2 %copy-start = (bf16[2048,512]{1,0:T(8,128)(2,1)S(1)}, bf16[2048,512]{1,0:T(8,128)(2,1)}, u32[]{:S(2)}) copy-start(bf16[2048,512]{1,0:T(8,128)(2,1)} %param.11) | copy-start | bytes 6291460
  10.3 12.2 %copy-start.1 = (bf16[128,2048]{1,0:T(8,128)(2,1)S(1)}, bf16[128,2048]{1,0:T(8,128)(2,1)}, u32[]{:S(2)}) copy-start(bf16[128,2048]{1,0:T(8,128)(2,1)} %param.10) | copy-start | bytes 1572868
  15.3 19.0 %all-to-all-start.1 = ((bf16[8,1,48,512]{3,2,1,0:T(8,128)(2,1)}), bf16[8,1,48,512]{3,2,1,0:T(8,128)(2,1)S(1)}, u32[]{:S(2)}, u32[]{:S(2)}) async-start(bf16[8,1,48,512]{3,2,1,0:T(8,128)(2,1)} %bitcast.12), calls=%async_computation.1 | async-start | bytes 786432 | tf_op jit(solution)/shard_map/all_to_all | solution.py:55
  34.3 15.2 %all-to-all-start = ((bf16[8,1,48,512]{3,2,1,0:T(8,128)(2,1)}), bf16[8,1,48,512]{3,2,1,0:T(8,128)(2,1)S(1)}, u32[]{:S(2)}, u32[]{:S(2)}) async-start(bf16[8,1,48,512]{3,2,1,0:T(8,128)(2,1)} %bitcast.5), calls=%async_computation | async-start | bytes 786432 | tf_op jit(solution)/shard_map/all_to_all | solution.py:58
  37.9 3.0 %copy-start.4 = (bf16[1,512,1024]{2,1,0:T(8,128)(2,1)S(1)}, bf16[1,512,1024]{2,1,0:T(8,128)(2,1)}, u32[]{:S(2)}) copy-start(bf16[1,512,1024]{2,1,0:T(8,128)(2,1)} %param.14) | copy-start | bytes 3145732
  49.5 2.0 %copy-start.2 = (f32[8,48,1024]{2,1,0:T(8,128)S(1)}, f32[8,48,1024]{2,1,0:T(8,128)}, u32[]{:S(2)}) copy-start(f32[8,48,1024]{2,1,0:T(8,128)} %fusion.18) | copy-start | bytes 4718596
  49.5 2.0 %copy-start.3 = (bf16[1,512,1024]{2,1,0:T(8,128)(2,1)S(1)}, bf16[1,512,1024]{2,1,0:T(8,128)(2,1)}, u32[]{:S(2)}) copy-start(bf16[1,512,1024]{2,1,0:T(8,128)(2,1)} %param.13) | copy-start | bytes 3145732
  51.5 2.5 %copy-start.5 = (bf16[1,512,1024]{2,1,0:T(8,128)(2,1)S(1)}, bf16[1,512,1024]{2,1,0:T(8,128)(2,1)}, u32[]{:S(2)}) copy-start(bf16[1,512,1024]{2,1,0:T(8,128)(2,1)} %param.14) | copy-start | bytes 3145732
  54.0 5.0 %copy-start.6 = (bf16[1,1024,512]{2,1,0:T(8,128)(2,1)S(1)}, bf16[1,1024,512]{2,1,0:T(8,128)(2,1)}, u32[]{:S(2)}) copy-start(bf16[1,1024,512]{2,1,0:T(8,128)(2,1)} %param.15) | copy-start | bytes 3145732
  55.4 14.7 %all-to-all-start.2 = ((bf16[8,1,48,512]{3,2,1,0:T(8,128)(2,1)}), bf16[8,1,48,512]{3,2,1,0:T(8,128)(2,1)S(1)}, u32[]{:S(2)}, u32[]{:S(2)}) async-start(bf16[8,1,48,512]{3,2,1,0:T(8,128)(2,1)} %fusion.12), calls=%async_computation.2 | async-start | bytes 786432 | tf_op jit(solution)/shard_map/all_to_all | solution.py:60
  59.0 15.0 %copy-start.7 = (f32[128,2]{0,1:T(2,128)S(1)}, f32[128,2]{0,1:T(2,128)}, u32[]{:S(2)}) copy-start(f32[128,2]{0,1:T(2,128)} %param.16) | copy-start | bytes 3076
  70.1 14.8 %all-to-all-start.3 = ((bf16[8,1,48,512]{3,2,1,0:T(8,128)(2,1)}), bf16[8,1,48,512]{3,2,1,0:T(8,128)(2,1)S(1)}, u32[]{:S(2)}, u32[]{:S(2)}) async-start(bf16[8,1,48,512]{3,2,1,0:T(8,128)(2,1)} %fusion.11), calls=%async_computation.3 | async-start | bytes 786432 | tf_op jit(solution)/shard_map/all_to_all | solution.py:57
  73.8 65.2 %reduce-scatter.2.cloned.1.call-start = ((), (), s32[]{:S(2)}) async-start(), calls=%async_computation.5 | async-start | bytes 5242880 | tf_op jit(solution)/shard_map/reduce_scatter | solution.py:75
Sparse Core Ops, SparseCore 0:
  95.4 43.5 reduce-scatter.1
where the time goes:
time: 151 us; the launch traced here: 150 us
  waiting for transfers between devices  68.8 us (46%)
  matrix products  24.5 us (16%)
  starting transfers between devices  18.4 us (12%)
  local copies, waits for them, and re-layouts  17.7 us (12%)
  between operations  14.2 us (9%)
  other arithmetic  6.19 us (4%)
    reduce_scatter x1, waiting for transfers between devices, body(): lax.psum_scatter(jnp.einsum('btc,btl->cbl', paired_left, paired_right, pr...  41.4 us
    all_to_all x1, waiting for transfers between devices, body(): lax.all_to_all(grad_z, 'expert', split_axis=0, concat_axis=0, tiled=True)  7.87 us
    all_to_all x1, waiting for transfers between devices, body(): lax.all_to_all(outv, 'expert', split_axis=0, concat_axis=0, tiled=True)  7.55 us
    all_to_all x1, starting transfers between devices, body(): lax.all_to_all(z_send, 'expert', split_axis=0, concat_axis=0, tiled=True)  7.28 us
    all_to_all x1, waiting for transfers between devices, body(): lax.all_to_all(g_send, 'expert', split_axis=0, concat_axis=0, tiled=True)  6.81 us
    scatter x2, local copies, waits for them, and re-layouts, body(): jnp.zeros((experts * capacity, width_lat), jnp.bfloat16).at[position]  6.77 us
    all_to_all x1, waiting for transfers between devices, body(): lax.all_to_all(z_send, 'expert', split_axis=0, concat_axis=0, tiled=True)  5.16 us
    dot_general x1, matrix products, body(): jnp.einsum('btc,btl->cbl', paired_left, paired_right, preferred_element_t...  4.37 us
  transfers between devices with their start and end apart: 5, of which 5 were waited for; matrix products, arithmetic and copies ran while one was open for 13% of the time, Pallas kernels for 0%

commit v1 on v0

v1 whole, which is shorter than its diff:
```python
import functools

import jax
import jax.numpy as jnp
from jax import lax
from jax.experimental import pallas as pl
from jax.experimental.pallas import tpu as pltpu
from jax.sharding import PartitionSpec as P

BF16 = jnp.bfloat16
F32 = jnp.float32
MESH = pl.DeviceIdType.MESH


def dot(a, b, ca=1, cb=0):
    return lax.dot_general(a, b, (((ca,), (cb,)), ((), ())), preferred_element_type=F32)


def flip(me, k, n):
    out, bit = 0, 1
    while bit < n:
        mine = lax.rem(me // bit, 2)
        out = out + (1 - mine if (k // bit) % 2 else mine) * bit
        bit *= 2
    return out


def kernel(
    n_e, n_dp, cap,
    tokens_h, dy_h, w_in_h, w_out_h, wg_h, wu_h, wd_h, logits, ids,
    tg_h, logit_grad, gin_h, gout_h,
    tokens, dy, w_in, w_out, wg, wu, wd,
    q, lat_grad,
    z_send, g_send, o_send, c_send, z_recv, g_recv, o_recv, c_recv,
    pre_a, pre_b, hid, ga, gb,
    tok_all, dy_all, mix_all, lg_all,
    tg, gin, gout,
    load_sem, own_sem, ssem, rsem, tssem, trsem, mssem, mrsem, lssem, lrsem, out_sem,
):
    rows, top = ids.shape
    slots = n_e * cap
    lat = w_in.shape[1]
    hidden = wg.shape[1]
    dw = tok_all.shape[1]
    me = lax.axis_index("expert")
    dp = lax.axis_index("dp")
    n_x = n_dp // 2
    x, c = dp // 2, lax.rem(dp, 2)

    loads = []
    for i, (src, dst) in enumerate((
        (tokens_h, tokens), (w_in_h, w_in), (dy_h, dy), (w_out_h, w_out),
        (wg_h.at[0], wg), (wu_h.at[0], wu), (wd_h.at[0], wd),
    )):
        load = pltpu.make_async_copy(src, dst, load_sem.at[i])
        load.start()
        loads.append(load)

    barrier = pltpu.get_barrier_semaphore()
    for k in range(1, n_e):
        pl.semaphore_signal(barrier, inc=1, device_id={"expert": flip(me, k, n_e)}, device_id_type=MESH)
    for k in range(1, n_dp):
        pl.semaphore_signal(barrier, inc=1, device_id={"dp": lax.rem(dp + k, n_dp)}, device_id_type=MESH)

    wide = -(-n_e // 128) * 128
    idv = ids[...]
    lane = lax.broadcasted_iota(jnp.int32, (rows, wide), 1)
    hots = [(idv[:, k:k + 1] == lane).astype(F32) for k in range(top)]
    below = lax.broadcasted_iota(jnp.int32, (rows, rows), 1) < lax.broadcasted_iota(jnp.int32, (rows, rows), 0)
    rank = dot(below.astype(BF16), sum(hots[1:], hots[0]).astype(BF16))
    slot_lane = lax.broadcasted_iota(jnp.int32, (rows, slots), 1)
    both = jnp.zeros((rows, slots), F32)
    for k in range(top):
        slot = jnp.sum(hots[k] * rank, axis=1, keepdims=True).astype(jnp.int32)
        hit = (slot_lane == idv[:, k:k + 1] * cap + slot).astype(F32)
        q[k] = hit.astype(BF16)
        both = both + hit
    spread = both.T.astype(BF16)
    score = jax.nn.sigmoid(logits[...])
    total = jnp.sum(score, axis=1, keepdims=True)
    gate = score / total

    pieces = [pl.ds(pl.multiple_of(flip(me, k, n_e) * cap, cap), cap) for k in range(n_e)]
    order = list(range(n_e - 1, 0, -1))

    def exchange(phase, src, dst):
        own = pltpu.make_async_copy(src.at[pieces[0]], dst.at[pieces[0]], own_sem.at[phase])
        copies = [
            pltpu.make_async_remote_copy(
                src_ref=src.at[pieces[k]], dst_ref=dst.at[pieces[0]],
                send_sem=ssem.at[phase, k], recv_sem=rsem.at[phase, k],
                device_id={"expert": flip(me, k, n_e)}, device_id_type=MESH,
            )
            for k in order
        ]
        for copy in copies:
            copy.start()
        own.start()
        return own, copies

    def arrived(pair):
        pair[0].wait()
        for copy in pair[1]:
            copy.wait_recv()

    def block(i):
        return pl.ds(pl.multiple_of(i * rows, rows), rows)

    loads[0].wait()
    loads[1].wait()
    latent = dot(tokens[...], w_in[...]).astype(BF16)
    z_send[...] = dot(spread, latent).astype(BF16)
    pl.semaphore_wait(barrier, n_e + n_dp - 2)
    z_pair = exchange(0, z_send, z_recv)
    loads[2].wait()
    loads[3].wait()
    lat_grad[...] = dot(dy[...], w_out[...], 1, 1).astype(BF16)
    g_send[...] = dot(spread, lat_grad[...]).astype(BF16)
    g_pair = exchange(1, g_send, g_recv)

    slices = []
    for k in range(1, n_dp):
        peer = lax.rem(dp + k, n_dp)
        cols = pl.ds(pl.multiple_of(peer * dw, dw), dw)
        for j, (src, dst) in enumerate(((tokens, tok_all), (dy, dy_all))):
            copy = pltpu.make_async_remote_copy(
                src_ref=src.at[:, cols], dst_ref=dst.at[block(dp)],
                send_sem=tssem.at[j, k], recv_sem=trsem.at[j, k],
                device_id={"dp": peer}, device_id_type=MESH,
            )
            copy.start()
            slices.append(copy)
    mine = pl.ds(pl.multiple_of(dp * dw, dw), dw)
    tok_all[block(dp), :] = tokens[:, mine]
    dy_all[block(dp), :] = dy[:, mine]

    tile = min(256, hidden)
    loads[4].wait()
    loads[5].wait()
    loads[6].wait()
    arrived(z_pair)
    for t in range(hidden // tile):
        cut = slice(t * tile, (t + 1) * tile)
        a = dot(z_recv[...], wg[:, cut])
        b = dot(z_recv[...], wu[:, cut])
        pre_a[:, cut] = a
        pre_b[:, cut] = b
        hid[:, cut] = (a * jax.nn.sigmoid(a) * b).astype(BF16)
    o_send[...] = dot(hid[...], wd[...]).astype(BF16)
    o_pair = exchange(2, o_send, o_recv)

    arrived(g_pair)
    for t in range(hidden // tile):
        cut = slice(t * tile, (t + 1) * tile)
        h = dot(g_recv[...], wd[cut, :], 1, 1)
        a, b = pre_a[:, cut], pre_b[:, cut]
        sg = jax.nn.sigmoid(a)
        ga[:, cut] = (h * b * sg * (1.0 + a * (1.0 - sg))).astype(BF16)
        gb[:, cut] = (h * a * sg).astype(BF16)
    c_send[...] = (dot(ga[...], wg[...], 1, 1) + dot(gb[...], wu[...], 1, 1)).astype(BF16)
    c_pair = exchange(3, c_send, c_recv)

    def share(buf, ss, rs):
        def send(origin, target, k):
            copy = pltpu.make_async_remote_copy(
                src_ref=buf.at[block(origin)], dst_ref=buf.at[block(origin)],
                send_sem=ss.at[k], recv_sem=rs.at[k],
                device_id={"dp": target}, device_id_type=MESH,
            )
            copy.start()
            return copy

        across = [send(dp, lax.rem(x + d, n_x) * 2 + c, d) for d in range(1, n_x)]
        pair = [send(dp, x * 2 + 1 - c, n_x)]
        return across, pair, send

    def pass_on(shared):
        across, pair, send = shared
        for d in range(1, n_x):
            across[d - 1].wait_recv()
            pair.append(send(lax.rem(x - d + n_x, n_x) * 2 + c, x * 2 + 1 - c, n_x + d))
        return across + pair

    arrived(o_pair)
    mixed = jnp.zeros((rows, lat), F32)
    lgf = lat_grad[...].astype(F32)
    gate_grads = []
    for k in range(top):
        back = dot(q[k], o_recv[...])
        mixed = mixed + gate[:, k:k + 1] * back
        gate_grads.append(jnp.sum(back * lgf, axis=1, keepdims=True))
    mix_all[block(dp), :] = mixed.astype(BF16)
    mix_share = share(mix_all, mssem, mrsem)
    mean = sum(gate[:, k:k + 1] * gate_grads[k] for k in range(top))
    column = lax.broadcasted_iota(jnp.int32, (rows, top), 1)
    gate_grad = jnp.zeros((rows, top), F32)
    for k in range(top):
        gate_grad = jnp.where(column == k, gate_grads[k], gate_grad)
    logit_grad[...] = score * (1.0 - score) * (gate_grad - mean) / total
    mix_sent = pass_on(mix_share)
    for copy in slices:
        copy.wait_recv()
    for copy in mix_sent[n_x - 1:]:
        copy.wait_recv()
    gout[...] = dot(mix_all[...], dy_all[...], 0, 0)
    out2 = pltpu.make_async_copy(gout, gout_h.at[0], out_sem.at[2])
    out2.start()

    arrived(c_pair)
    total_grad = jnp.zeros((rows, lat), F32)
    for k in range(top):
        total_grad = total_grad + gate[:, k:k + 1] * dot(q[k], c_recv[...])
    latent_grad = total_grad.astype(BF16)
    lg_all[block(dp), :] = latent_grad
    lg_share = share(lg_all, lssem, lrsem)
    tg[...] = dot(latent_grad, w_in[...], 1, 1).astype(BF16)
    out0 = pltpu.make_async_copy(tg, tg_h, out_sem.at[0])
    out0.start()
    lg_sent = pass_on(lg_share)
    for copy in lg_sent[n_x - 1:]:
        copy.wait_recv()
    gin[...] = dot(tok_all[...], lg_all[...], 0, 0)
    out1 = pltpu.make_async_copy(gin, gin_h.at[0], out_sem.at[1])
    out1.start()

    for pair in (z_pair, g_pair, o_pair, c_pair):
        for copy in pair[1]:
            copy.wait_send()
    for copy in slices + mix_sent + lg_sent:
        copy.wait_send()
    out2.wait()
    out0.wait()
    out1.wait()


def body(n_e, n_dp, tokens, out_grad, w_in, w_out, w_gate, w_up, w_down, gate_logits, expert_ids):
    rows, width = tokens.shape
    top = expert_ids.shape[1]
    lat = w_in.shape[1]
    hidden = w_gate.shape[2]
    assert w_gate.shape[0] == 1 and n_dp % 2 == 0
    cap = 3 * rows * top // (2 * n_e)
    cap = -(-cap // 16) * 16
    slots = n_e * cap
    dw = width // n_dp
    any_ = pl.BlockSpec(memory_space=pl.ANY)
    vmem = pl.BlockSpec(memory_space=pltpu.VMEM)
    V = pltpu.VMEM
    dma = pltpu.SemaphoreType.DMA
    return pl.pallas_call(
        functools.partial(kernel, n_e, n_dp, cap),
        out_shape=(
            jax.ShapeDtypeStruct((rows, width), BF16),
            jax.ShapeDtypeStruct((rows, top), F32),
            jax.ShapeDtypeStruct((1, dw, lat), F32),
            jax.ShapeDtypeStruct((1, lat, dw), F32),
        ),
        in_specs=[any_] * 7 + [vmem] * 2,
        out_specs=(any_, vmem, any_, any_),
        scratch_shapes=[
            V((rows, width), BF16), V((rows, width), BF16),
            V((width, lat), BF16), V((lat, width), BF16),
            V((lat, hidden), BF16), V((lat, hidden), BF16), V((hidden, lat), BF16),
            V((top, rows, slots), BF16), V((rows, lat), BF16),
            *[V((slots, lat), BF16)] * 8,
            V((slots, hidden), F32), V((slots, hidden), F32),
            V((slots, hidden), BF16), V((slots, hidden), BF16), V((slots, hidden), BF16),
            V((n_dp * rows, dw), BF16), V((n_dp * rows, dw), BF16),
            V((n_dp * rows, lat), BF16), V((n_dp * rows, lat), BF16),
            V((rows, width), BF16), V((dw, lat), F32), V((lat, dw), F32),
            dma((7,)), dma((4,)), dma((4, n_e)), dma((4, n_e)),
            dma((2, n_dp)), dma((2, n_dp)),
            dma((n_dp,)), dma((n_dp,)), dma((n_dp,)), dma((n_dp,)), dma((3,)),
        ],
        compiler_params=pltpu.CompilerParams(
            collective_id=0, has_side_effects=True, vmem_limit_bytes=56 * 1024 * 1024
        ),
    )(tokens, out_grad, w_in, w_out, w_gate, w_up, w_down, gate_logits, expert_ids)


def solution(mesh):
    placed = (
        P(("dp", "expert"), None),
        P(("dp", "expert"), None),
        P(),
        P(),
        P("expert", None, None),
        P("expert", None, None),
        P("expert", None, None),
        P(("dp", "expert"), None),
        P(("dp", "expert"), None),
    )
    return jax.shard_map(
        functools.partial(body, mesh.shape["expert"], mesh.shape["dp"]),
        mesh=mesh,
        in_specs=placed,
        out_specs=(
            P(("dp", "expert"), None),
            P(("dp", "expert"), None),
            P("expert", "dp", None),
            P("expert", None, "dp"),
        ),
        check_vma=False,
    )
```

time: 151 us -> 63.2 us (0.42)
  waiting for transfers between devices: 68.8 us -> 0 us
  Pallas kernels: 0 us -> 52.8 us
  matrix products: 24.5 us -> 0 us
  starting transfers between devices: 18.4 us -> 0 us
  between operations: 14.2 us -> 0.65 us
  local copies, waits for them, and re-layouts: 17.7 us -> 9.51 us
  other arithmetic: 6.19 us -> 0 us
    pallas_call x0 -> x1, Pallas kernels: none -> 52.8 us  [body(): pl.pallas_call(functools.partial(kernel, n_e, n_dp, cap), out_shape=(jax....]
    reduce_scatter x1 -> x0, waiting for transfers between devices: 41.4 us -> none  [body(): lax.psum_scatter(jnp.einsum('btc,btl->cbl', paired_left, paired_right, pr...]
    all_to_all x4 -> x0, waiting for transfers between devices: 27.4 us -> none  [the longest x1 7.87 us: body(): lax.all_to_all(grad_z, 'expert', split_axis=0, concat_axis=0, tiled=True)]
    dot_general x10 -> x0, matrix products: 24.5 us -> none  [the longest x1 4.37 us: body(): jnp.einsum('btc,btl->cbl', paired_left, paired_right, preferred_element_t...]
    all_to_all x4 -> x0, starting transfers between devices: 18.2 us -> none  [the longest x1 7.28 us: body(): lax.all_to_all(z_send, 'expert', split_axis=0, concat_axis=0, tiled=True)]
    scatter x2 -> x0, local copies, waits for them, and re-layouts: 6.77 us -> none  [body(): jnp.zeros((experts * capacity, width_lat), jnp.bfloat16).at[position]]
    unnamed x18 -> x7, local copies, waits for them, and re-layouts: 2.3 us -> 7.94 us
    gather x2 -> x0, local copies, waits for them, and re-layouts: 3.71 us -> none  [the longest x1 1.85 us: body(): back_grad[position].reshape(tok_rows, top, width_lat).astype(jnp.float32)]
  transfers between devices with their start and end apart: 5 -> 0, of which waited for: 5 -> 0; matrix products, arithmetic and copies ran while one was open for 13% -> 0% of each run, Pallas kernels for 0% -> 0%
where the time goes in v1:
time: 63.2 us; the launch traced here: 62.9 us
  Pallas kernels  52.8 us (84%)
  local copies, waits for them, and re-layouts  9.51 us (15%)
  between operations  0.65 us (1%)
    pallas_call x1, Pallas kernels, body(): pl.pallas_call(functools.partial(kernel, n_e, n_dp, cap), out_shape=(jax....  52.8 us
    unnamed x7, local copies, waits for them, and re-layouts  7.94 us
    pallas_call x1, local copies, waits for them, and re-layouts, body(): pl.pallas_call(functools.partial(kernel, n_e, n_dp, cap), out_shape=(jax....  1.56 us

profile of v1, /device:TPU:0, one launch (start us, length us, event | category | flops | bytes accessed | tf_op | source)
XLA Modules:
  0.0 62.9 jit_solution(2144051474317753619)
XLA Ops:
  0.6 1.4 %copy.13.logits = f32[128,2]{1,0:T(8,128)} copy(f32[128,2]{0,1:T(2,128)} %param.16) | data formatting | bytes 2048 | tf_op args[7]
  2.0 1.4 %copy.14.ids = s32[128,2]{1,0:T(8,128)} copy(s32[128,2]{0,1:T(2,128)} %param.17) | data formatting | bytes 2048 | tf_op args[8]
  3.5 52.8 %shard_map.120 = (bf16[128,2048]{1,0:T(8,128)(2,1)}, f32[128,2]{1,0:T(8,128)}, f32[1,512,512]{2,1,0:T(8,128)}, f32[1,512,512]{2,1,0:T(8,128)}) custom-call(bf16[128,2048]{1,0:T(8,128)(2,1)} %tokens_h.1, bf16[128,2048]{1,0:T(8,128)(2,1)} %dy_h.1, bf16[2048,512]{1,0:T(8,128)(2,1)} %w_in_h.1, bf16[512,2048]{1,0:T(8,128)(2,1)} %w_out_h.1, ...), custom_call_target="tpu_custom_call" | custom-call | tf_op jit(solution)/shard_map/pallas_call | solution.py:250
  56.2 0.0 copy-start
  56.2 1.6 %copy.15 = f32[128,2]{0,1:T(2,128)} copy(f32[128,2]{1,0:T(8,128)} %get-tuple-element.5) | data formatting | bytes 2048 | tf_op jit(solution)/shard_map/pallas_call | solution.py:250
  57.8 1.9 %copy.19 = bf16[128,2048]{1,0:T(8,128)(2,1)} copy(bf16[128,2048]{1,0:T(8,128)(2,1)} %get-tuple-element.12) | data formatting | bytes 1048576
  59.7 2.3 %copy.20 = f32[1,512,512]{2,1,0:T(8,128)} copy(f32[1,512,512]{2,1,0:T(8,128)} %get-tuple-element.14) | data formatting | bytes 2097152
  61.9 0.0 copy-done
  62.0 1.0 %copy.21 = f32[1,512,512]{2,1,0:T(8,128)} copy(f32[1,512,512]{2,1,0:T(8,128)S(1)} %copy-done) | data formatting | bytes 2097152
Async XLA Ops:
  56.2 5.7 %copy-start = (f32[1,512,512]{2,1,0:T(8,128)S(1)}, f32[1,512,512]{2,1,0:T(8,128)}, u32[]{:S(2)}) copy-start(f32[1,512,512]{2,1,0:T(8,128)} %get-tuple-element.15) | copy-start | bytes 3145732

commit v2 on v1

--- a/solution.py
+++ b/solution.py
@@ -28,16 +28,15 @@
 def kernel(
     n_e, n_dp, cap,
     tokens_h, dy_h, w_in_h, w_out_h, wg_h, wu_h, wd_h, logits, ids,
-    tg_h, logit_grad, gin_h, gout_h,
+    logit_grad, tok_all, dy_all, mix_all, lg_all,
     tokens, dy, w_in, w_out, wg, wu, wd,
     q, lat_grad,
     z_send, g_send, o_send, c_send, z_recv, g_recv, o_recv, c_recv,
     pre_a, pre_b, hid, ga, gb,
-    tok_all, dy_all, mix_all, lg_all,
-    tg, gin, gout,
+    mix, lg,
     load_sem, own_sem, ssem, rsem, tssem, trsem, mssem, mrsem, lssem, lrsem, out_sem,
 ):
-    rows, top = ids.shape
+    top, rows = ids.shape
     slots = n_e * cap
     lat = w_in.shape[1]
     hidden = wg.shape[1]
@@ -62,23 +61,18 @@
     for k in range(1, n_dp):
         pl.semaphore_signal(barrier, inc=1, device_id={"dp": lax.rem(dp + k, n_dp)}, device_id_type=MESH)
 
-    wide = -(-n_e // 128) * 128
     idv = ids[...]
-    lane = lax.broadcasted_iota(jnp.int32, (rows, wide), 1)
-    hots = [(idv[:, k:k + 1] == lane).astype(F32) for k in range(top)]
-    below = lax.broadcasted_iota(jnp.int32, (rows, rows), 1) < lax.broadcasted_iota(jnp.int32, (rows, rows), 0)
-    rank = dot(below.astype(BF16), sum(hots[1:], hots[0]).astype(BF16))
-    slot_lane = lax.broadcasted_iota(jnp.int32, (rows, slots), 1)
-    both = jnp.zeros((rows, slots), F32)
+    tall = -(-n_e // 16) * 16
+    level = lax.broadcasted_iota(jnp.int32, (tall, rows), 0)
+    hots = [(level == idv[k:k + 1, :]).astype(F32) for k in range(top)]
+    above = lax.broadcasted_iota(jnp.int32, (rows, rows), 0) < lax.broadcasted_iota(jnp.int32, (rows, rows), 1)
+    rank = dot(sum(hots[1:], hots[0]).astype(BF16), above.astype(BF16))
+    slot_level = lax.broadcasted_iota(jnp.int32, (slots, rows), 0)
+    where = []
     for k in range(top):
-        slot = jnp.sum(hots[k] * rank, axis=1, keepdims=True).astype(jnp.int32)
-        hit = (slot_lane == idv[:, k:k + 1] * cap + slot).astype(F32)
-        q[k] = hit.astype(BF16)
-        both = both + hit
-    spread = both.T.astype(BF16)
-    score = jax.nn.sigmoid(logits[...])
-    total = jnp.sum(score, axis=1, keepdims=True)
-    gate = score / total
+        slot = jnp.sum(hots[k] * rank, axis=0, keepdims=True).astype(jnp.int32)
+        where.append((slot_level == idv[k:k + 1, :] * cap + slot).astype(F32))
+    spread = sum(where[1:], where[0]).astype(BF16)
 
     pieces = [pl.ds(pl.multiple_of(flip(me, k, n_e) * cap, cap), cap) for k in range(n_e)]
     order = list(range(n_e - 1, 0, -1))
@@ -131,8 +125,18 @@
             copy.start()
             slices.append(copy)
     mine = pl.ds(pl.multiple_of(dp * dw, dw), dw)
-    tok_all[block(dp), :] = tokens[:, mine]
-    dy_all[block(dp), :] = dy[:, mine]
+    keep = []
+    for j, (src, dst) in enumerate(((tokens, tok_all), (dy, dy_all))):
+        copy = pltpu.make_async_copy(src.at[:, mine], dst.at[block(dp)], out_sem.at[j])
+        copy.start()
+        keep.append(copy)
+
+    for k in range(top):
+        q[k] = where[k].T.astype(BF16)
+    score = jax.nn.sigmoid(logits[...])
+    total = jnp.sum(score, axis=0, keepdims=True)
+    gate = score / total
+    gate_col = jnp.concatenate([gate, jnp.zeros((128 - top, rows), F32)], axis=0).T
 
     tile = min(256, hidden)
     loads[4].wait()
@@ -160,10 +164,14 @@
     c_send[...] = (dot(ga[...], wg[...], 1, 1) + dot(gb[...], wu[...], 1, 1)).astype(BF16)
     c_pair = exchange(3, c_send, c_recv)
 
-    def share(buf, ss, rs):
+    def share(own, buf, ss, rs, slot):
+        copy = pltpu.make_async_copy(own, buf.at[block(dp)], out_sem.at[slot])
+        copy.start()
+        keep.append(copy)
+
         def send(origin, target, k):
             copy = pltpu.make_async_remote_copy(
-                src_ref=buf.at[block(origin)], dst_ref=buf.at[block(origin)],
+                src_ref=own if k <= n_x else buf.at[block(origin)], dst_ref=buf.at[block(origin)],
                 send_sem=ss.at[k], recv_sem=rs.at[k],
                 device_id={"dp": target}, device_id_type=MESH,
             )
@@ -184,53 +192,70 @@
     arrived(o_pair)
     mixed = jnp.zeros((rows, lat), F32)
     lgf = lat_grad[...].astype(F32)
-    gate_grads = []
+    lane = lax.broadcasted_iota(jnp.int32, (rows, 128), 1)
+    gate_grad = jnp.zeros((rows, 128), F32)
     for k in range(top):
         back = dot(q[k], o_recv[...])
-        mixed = mixed + gate[:, k:k + 1] * back
-        gate_grads.append(jnp.sum(back * lgf, axis=1, keepdims=True))
-    mix_all[block(dp), :] = mixed.astype(BF16)
-    mix_share = share(mix_all, mssem, mrsem)
-    mean = sum(gate[:, k:k + 1] * gate_grads[k] for k in range(top))
-    column = lax.broadcasted_iota(jnp.int32, (rows, top), 1)
-    gate_grad = jnp.zeros((rows, top), F32)
-    for k in range(top):
-        gate_grad = jnp.where(column == k, gate_grads[k], gate_grad)
+        mixed = mixed + gate_col[:, k:k + 1] * back
+        gate_grad = jnp.where(lane == k, jnp.sum(back * lgf, axis=1, keepdims=True), gate_grad)
+    mix[...] = mixed.astype(BF16)
+    mix_share = share(mix, mix_all, mssem, mrsem, 2)
+    gate_grad = gate_grad.T[:top, :]
+    mean = jnp.sum(gate * gate_grad, axis=0, keepdims=True)
     logit_grad[...] = score * (1.0 - score) * (gate_grad - mean) / total
     mix_sent = pass_on(mix_share)
-    for copy in slices:
-        copy.wait_recv()
-    for copy in mix_sent[n_x - 1:]:
-        copy.wait_recv()
-    gout[...] = dot(mix_all[...], dy_all[...], 0, 0)
-    out2 = pltpu.make_async_copy(gout, gout_h.at[0], out_sem.at[2])
-    out2.start()
 
     arrived(c_pair)
     total_grad = jnp.zeros((rows, lat), F32)
     for k in range(top):
-        total_grad = total_grad + gate[:, k:k + 1] * dot(q[k], c_recv[...])
-    latent_grad = total_grad.astype(BF16)
-    lg_all[block(dp), :] = latent_grad
-    lg_share = share(lg_all, lssem, lrsem)
-    tg[...] = dot(latent_grad, w_in[...], 1, 1).astype(BF16)
-    out0 = pltpu.make_async_copy(tg, tg_h, out_sem.at[0])
-    out0.start()
-    lg_sent = pass_on(lg_share)
-    for copy in lg_sent[n_x - 1:]:
+        total_grad = total_grad + gate_col[:, k:k + 1] * dot(q[k], c_recv[...])
+    lg[...] = total_grad.astype(BF16)
+    lg_sent = pass_on(share(lg, lg_all, lssem, lrsem, 3))
+
+    for copy in slices + mix_sent[n_x - 1:] + lg_sent[n_x - 1:]:
         copy.wait_recv()
-    gin[...] = dot(tok_all[...], lg_all[...], 0, 0)
-    out1 = pltpu.make_async_copy(gin, gin_h.at[0], out_sem.at[1])
-    out1.start()
-
     for pair in (z_pair, g_pair, o_pair, c_pair):
         for copy in pair[1]:
             copy.wait_send()
     for copy in slices + mix_sent + lg_sent:
         copy.wait_send()
-    out2.wait()
-    out0.wait()
-    out1.wait()
+    for copy in keep:
+        copy.wait()
+
+
+def last_kernel(
+    n_dp, w_in_h, tok_h, dy_h, mix_h, lg_h, part, tg_h, gin_h, gout_h, logit_grad,
+    w_in, tok, dy, mix, lg, tg, gin, gout, sem, out_sem,
+):
+    rows = tg.shape[0]
+    loads = []
+    for i, (src, dst) in enumerate(((dy_h, dy), (mix_h, mix), (tok_h, tok), (lg_h, lg), (w_in_h, w_in))):
+        copy = pltpu.make_async_copy(src, dst, sem.at[i])
+        copy.start()
+        loads.append(copy)
+    logit_grad[...] = part[...]
+    dp = lax.axis_index("dp")
+    stores = []
+
+    def store(src, dst):
+        copy = pltpu.make_async_copy(src, dst, out_sem.at[len(stores)])
+        copy.start()
+        stores.append(copy)
+
+    loads[0].wait()
+    loads[1].wait()
+    gout[...] = dot(mix[...], dy[...], 0, 0)
+    store(gout, gout_h.at[0])
+    loads[2].wait()
+    loads[3].wait()
+    gin[...] = dot(tok[...], lg[...], 0, 0)
+    store(gin, gin_h.at[0])
+    loads[4].wait()
+    own = lg[pl.ds(pl.multiple_of(dp * rows, rows), rows), :]
+    tg[...] = dot(own, w_in[...], 1, 1).astype(BF16)
+    store(tg, tg_h)
+    for copy in stores:
+        copy.wait()
 
 
 def body(n_e, n_dp, tokens, out_grad, w_in, w_out, w_gate, w_up, w_down, gate_logits, expert_ids):
@@ -247,16 +272,17 @@
     vmem = pl.BlockSpec(memory_space=pltpu.VMEM)
     V = pltpu.VMEM
     dma = pltpu.SemaphoreType.DMA
-    return pl.pallas_call(
+    arrays = pl.pallas_call(
         functools.partial(kernel, n_e, n_dp, cap),
         out_shape=(
-            jax.ShapeDtypeStruct((rows, width), BF16),
-            jax.ShapeDtypeStruct((rows, top), F32),
-            jax.ShapeDtypeStruct((1, dw, lat), F32),
-            jax.ShapeDtypeStruct((1, lat, dw), F32),
+            jax.ShapeDtypeStruct((top, rows), F32),
+            jax.ShapeDtypeStruct((n_dp * rows, dw), BF16),
+            jax.ShapeDtypeStruct((n_dp * rows, dw), BF16),
+            jax.ShapeDtypeStruct((n_dp * rows, lat), BF16),
+            jax.ShapeDtypeStruct((n_dp * rows, lat), BF16),
         ),
         in_specs=[any_] * 7 + [vmem] * 2,
-        out_specs=(any_, vmem, any_, any_),
+        out_specs=(vmem, any_, any_, any_, any_),
         scratch_shapes=[
             V((rows, width), BF16), V((rows, width), BF16),
             V((width, lat), BF16), V((lat, width), BF16),
@@ -265,17 +291,35 @@
             *[V((slots, lat), BF16)] * 8,
             V((slots, hidden), F32), V((slots, hidden), F32),
             V((slots, hidden), BF16), V((slots, hidden), BF16), V((slots, hidden), BF16),
+            V((rows, lat), BF16), V((rows, lat), BF16),
+            dma((7,)), dma((4,)), dma((4, n_e)), dma((4, n_e)),
+            dma((2, n_dp)), dma((2, n_dp)),
+            dma((n_dp,)), dma((n_dp,)), dma((n_dp,)), dma((n_dp,)), dma((4,)),
+        ],
+        compiler_params=pltpu.CompilerParams(
+            collective_id=0, has_side_effects=True, vmem_limit_bytes=48 * 1024 * 1024
+        ),
+    )(tokens, out_grad, w_in, w_out, w_gate, w_up, w_down, gate_logits.T, expert_ids.T)
+    token_grad, grad_in, grad_out, logit_grad = pl.pallas_call(
+        functools.partial(last_kernel, n_dp),
+        out_shape=(
+            jax.ShapeDtypeStruct((rows, width), BF16),
+            jax.ShapeDtypeStruct((1, dw, lat), F32),
+            jax.ShapeDtypeStruct((1, lat, dw), F32),
+            jax.ShapeDtypeStruct((top, rows), F32),
+        ),
+        in_specs=[any_] * 5 + [vmem],
+        out_specs=(any_, any_, any_, vmem),
+        scratch_shapes=[
+            V((width, lat), BF16),
             V((n_dp * rows, dw), BF16), V((n_dp * rows, dw), BF16),
             V((n_dp * rows, lat), BF16), V((n_dp * rows, lat), BF16),
             V((rows, width), BF16), V((dw, lat), F32), V((lat, dw), F32),
-            dma((7,)), dma((4,)), dma((4, n_e)), dma((4, n_e)),
-            dma((2, n_dp)), dma((2, n_dp)),
-            dma((n_dp,)), dma((n_dp,)), dma((n_dp,)), dma((n_dp,)), dma((3,)),
+            dma((5,)), dma((3,)),
         ],
-        compiler_params=pltpu.CompilerParams(
-            collective_id=0, has_side_effects=True, vmem_limit_bytes=56 * 1024 * 1024
-        ),
-    )(tokens, out_grad, w_in, w_out, w_gate, w_up, w_down, gate_logits, expert_ids)
+        compiler_params=pltpu.CompilerParams(vmem_limit_bytes=24 * 1024 * 1024),
+    )(w_in, *arrays[1:], arrays[0])
+    return token_grad, logit_grad.T, grad_in, grad_out
 
 
 def solution(mesh):

time: 63.2 us -> 59.2 us (0.937)
  local copies, waits for them, and re-layouts: 9.51 us -> 5.88 us
    pallas_call x1, Pallas kernels: 52.8 us -> 48.8 us  [body(): pl.pallas_call(functools.partial(kernel, n_e, n_dp, cap), out_shape=(jax....]
    pallas_call x0 -> x1, Pallas kernels: none -> 3.47 us  [body(): pl.pallas_call(functools.partial(last_kernel, n_dp), out_shape=(jax.Shape...]
    unnamed x7 -> x14, local copies, waits for them, and re-layouts: 7.94 us -> 5.88 us
    pallas_call x1 -> x0, local copies, waits for them, and re-layouts: 1.56 us -> none  [body(): pl.pallas_call(functools.partial(kernel, n_e, n_dp, cap), out_shape=(jax....]
where the time goes in v2:
time: 59.2 us; the launch traced here: 58.8 us
  Pallas kernels  52.3 us (88%)
  local copies, waits for them, and re-layouts  5.88 us (10%)
  between operations  0.66 us (1%)
    pallas_call x1, Pallas kernels, body(): pl.pallas_call(functools.partial(kernel, n_e, n_dp, cap), out_shape=(jax....  48.8 us
    unnamed x14, local copies, waits for them, and re-layouts  5.88 us
    pallas_call x1, Pallas kernels, body(): pl.pallas_call(functools.partial(last_kernel, n_dp), out_shape=(jax.Shape...  3.47 us

profile of v2, /device:TPU:0, one launch (start us, length us, event | category | flops | bytes accessed | tf_op | source)
XLA Modules:
  0.0 58.8 jit_solution(11123549461367897566)
XLA Ops:
  0.6 0.0 copy-start.1
  0.6 1.2 %copy-done.1 = bf16[1,512,1024]{2,1,0:T(8,128)(2,1)S(1)} copy-done((bf16[1,512,1024]{2,1,0:T(8,128)(2,1)S(1)}, bf16[1,512,1024]{2,1,0:T(8,128)(2,1)}, u32[]{:S(2)}) %copy-start.1) | copy-done | bytes 1048600
  1.9 0.0 copy-start.2
  1.9 1.2 %copy-done.2 = bf16[1,512,1024]{2,1,0:T(8,128)(2,1)S(1)} copy-done((bf16[1,512,1024]{2,1,0:T(8,128)(2,1)S(1)}, bf16[1,512,1024]{2,1,0:T(8,128)(2,1)}, u32[]{:S(2)}) %copy-start.2) | copy-done | bytes 1048600
  3.1 0.0 copy-start.3
  3.1 1.0 %copy-done.3 = bf16[128,2048]{1,0:T(8,128)(2,1)S(1)} copy-done((bf16[128,2048]{1,0:T(8,128)(2,1)S(1)}, bf16[128,2048]{1,0:T(8,128)(2,1)}, u32[]{:S(2)}) %copy-start.3) | copy-done | bytes 524312
  4.1 0.0 copy-start.4
  4.1 1.0 %copy-done.4 = bf16[128,2048]{1,0:T(8,128)(2,1)S(1)} copy-done((bf16[128,2048]{1,0:T(8,128)(2,1)S(1)}, bf16[128,2048]{1,0:T(8,128)(2,1)}, u32[]{:S(2)}) %copy-start.4) | copy-done | bytes 524312
  5.2 0.0 copy-start.5
  5.2 0.7 %copy-done.5 = f32[128,2]{0,1:T(2,128)S(1)} copy-done((f32[128,2]{0,1:T(2,128)S(1)}, f32[128,2]{0,1:T(2,128)}, u32[]{:S(2)}) %copy-start.5) | copy-done | bytes 1048
  5.8 0.0 copy-start.6
  5.9 0.7 %copy-done.6 = s32[128,2]{0,1:T(2,128)S(1)} copy-done((s32[128,2]{0,1:T(2,128)S(1)}, s32[128,2]{0,1:T(2,128)}, u32[]{:S(2)}) %copy-start.6) | copy-done | bytes 1048
  6.5 0.0 copy-start
  6.5 48.8 %shard_map.120 = (f32[2,128]{1,0:T(2,128)S(1)}, bf16[512,512]{1,0:T(8,128)(2,1)S(1)}, bf16[512,512]{1,0:T(8,128)(2,1)S(1)}, bf16[512,512]{1,0:T(8,128)(2,1)S(1)}, bf16[512,512]{1,0:T(8,128)(2,1)S(1)}) custom-call(bf16[128,2048]{1,0:T(8,128)(2,1)S(1)} %copy-done.3, bf16[128,2048]{1,0:T(8,128)(2,1)S(1)} %copy-done.4, bf16[2048,512]{1,0:T(8,128)(2,1)} %w_in_h.3, ...), custom_call_target="tpu_custom_call" | custom-call | tf_op jit(solution)/shard_map/pallas_call | solution.py:275
  55.4 0.0 copy-done
  55.4 3.5 %shard_map.121 = (bf16[128,2048]{1,0:T(8,128)(2,1)}, f32[1,512,512]{2,1,0:T(8,128)}, f32[1,512,512]{2,1,0:T(8,128)}, f32[2,128]{1,0:T(2,128)}) custom-call(bf16[2048,512]{1,0:T(8,128)(2,1)S(1)} %copy-done, bf16[512,512]{1,0:T(8,128)(2,1)S(1)} %get-tuple-element.13.tok_h, bf16[512,512]{1,0:T(8,128)(2,1)S(1)} %get-tuple-element.14.dy_h, ...), custom_call_target="tpu_custom_call" | custom-call | tf_op jit(solution)/shard_map/pallas_call | solution.py:303
Async XLA Ops:
  0.6 1.2 %copy-start.1 = (bf16[1,512,1024]{2,1,0:T(8,128)(2,1)S(1)}, bf16[1,512,1024]{2,1,0:T(8,128)(2,1)}, u32[]{:S(2)}) copy-start(bf16[1,512,1024]{2,1,0:T(8,128)(2,1)} %wg_h.1) | copy-start | bytes 3145732
  1.9 1.2 %copy-start.2 = (bf16[1,512,1024]{2,1,0:T(8,128)(2,1)S(1)}, bf16[1,512,1024]{2,1,0:T(8,128)(2,1)}, u32[]{:S(2)}) copy-start(bf16[1,512,1024]{2,1,0:T(8,128)(2,1)} %wu_h.1) | copy-start | bytes 3145732
  3.1 1.0 %copy-start.3 = (bf16[128,2048]{1,0:T(8,128)(2,1)S(1)}, bf16[128,2048]{1,0:T(8,128)(2,1)}, u32[]{:S(2)}) copy-start(bf16[128,2048]{1,0:T(8,128)(2,1)} %tokens_h.1) | copy-start | bytes 1572868
  4.1 1.0 %copy-start.4 = (bf16[128,2048]{1,0:T(8,128)(2,1)S(1)}, bf16[128,2048]{1,0:T(8,128)(2,1)}, u32[]{:S(2)}) copy-start(bf16[128,2048]{1,0:T(8,128)(2,1)} %dy_h.1) | copy-start | bytes 1572868
  5.2 0.7 %copy-start.5 = (f32[128,2]{0,1:T(2,128)S(1)}, f32[128,2]{0,1:T(2,128)}, u32[]{:S(2)}) copy-start(f32[128,2]{0,1:T(2,128)} %param.16) | copy-start | bytes 3076
  5.8 0.7 %copy-start.6 = (s32[128,2]{0,1:T(2,128)S(1)}, s32[128,2]{0,1:T(2,128)}, u32[]{:S(2)}) copy-start(s32[128,2]{0,1:T(2,128)} %param.17) | copy-start | bytes 3076
  6.5 48.8 %copy-start = (bf16[2048,512]{1,0:T(8,128)(2,1)S(1)}, bf16[2048,512]{1,0:T(8,128)(2,1)}, u32[]{:S(2)}) copy-start(bf16[2048,512]{1,0:T(8,128)(2,1)} %w_in_h.3) | copy-start | bytes 6291460

commit v3 on v2

--- a/solution.py
+++ b/solution.py
@@ -27,13 +27,13 @@
 
 def kernel(
     n_e, n_dp, cap,
-    tokens_h, dy_h, w_in_h, w_out_h, wg_h, wu_h, wd_h, logits, ids,
+    tokens_h, dy_h, w_in_h, w_out_h, wg_h, wu_h, wd_h, logits_h, ids_h,
     logit_grad, tok_all, dy_all, mix_all, lg_all,
     tokens, dy, w_in, w_out, wg, wu, wd,
     q, lat_grad,
     z_send, g_send, o_send, c_send, z_recv, g_recv, o_recv, c_recv,
     pre_a, pre_b, hid, ga, gb,
-    mix, lg,
+    mix, lg, logits, ids,
     load_sem, own_sem, ssem, rsem, tssem, trsem, mssem, mrsem, lssem, lrsem, out_sem,
 ):
     top, rows = ids.shape
@@ -48,11 +48,12 @@
 
     loads = []
     for i, (src, dst) in enumerate((
-        (tokens_h, tokens), (w_in_h, w_in), (dy_h, dy), (w_out_h, w_out),
+        (ids_h, ids), (logits_h, logits), (tokens_h, tokens), (w_in_h, w_in), (dy_h, dy), (w_out_h, w_out),
         (wg_h.at[0], wg), (wu_h.at[0], wu), (wd_h.at[0], wd),
     )):
         load = pltpu.make_async_copy(src, dst, load_sem.at[i])
-        load.start()
+        if i < 4:
+            load.start()
         loads.append(load)
 
     barrier = pltpu.get_barrier_semaphore()
@@ -61,6 +62,7 @@
     for k in range(1, n_dp):
         pl.semaphore_signal(barrier, inc=1, device_id={"dp": lax.rem(dp + k, n_dp)}, device_id_type=MESH)
 
+    loads[0].wait()
     idv = ids[...]
     tall = -(-n_e // 16) * 16
     level = lax.broadcasted_iota(jnp.int32, (tall, rows), 0)
@@ -100,14 +102,16 @@
     def block(i):
         return pl.ds(pl.multiple_of(i * rows, rows), rows)
 
-    loads[0].wait()
-    loads[1].wait()
+    loads[2].wait()
+    loads[3].wait()
+    for load in loads[4:]:
+        load.start()
     latent = dot(tokens[...], w_in[...]).astype(BF16)
     z_send[...] = dot(spread, latent).astype(BF16)
     pl.semaphore_wait(barrier, n_e + n_dp - 2)
     z_pair = exchange(0, z_send, z_recv)
-    loads[2].wait()
-    loads[3].wait()
+    loads[4].wait()
+    loads[5].wait()
     lat_grad[...] = dot(dy[...], w_out[...], 1, 1).astype(BF16)
     g_send[...] = dot(spread, lat_grad[...]).astype(BF16)
     g_pair = exchange(1, g_send, g_recv)
@@ -133,15 +137,16 @@
 
     for k in range(top):
         q[k] = where[k].T.astype(BF16)
+    loads[1].wait()
     score = jax.nn.sigmoid(logits[...])
     total = jnp.sum(score, axis=0, keepdims=True)
     gate = score / total
     gate_col = jnp.concatenate([gate, jnp.zeros((128 - top, rows), F32)], axis=0).T
 
     tile = min(256, hidden)
-    loads[4].wait()
-    loads[5].wait()
     loads[6].wait()
+    loads[7].wait()
+    loads[8].wait()
     arrived(z_pair)
     for t in range(hidden // tile):
         cut = slice(t * tile, (t + 1) * tile)
@@ -269,6 +274,7 @@
     slots = n_e * cap
     dw = width // n_dp
     any_ = pl.BlockSpec(memory_space=pl.ANY)
+    hbm = pl.BlockSpec(memory_space=pltpu.HBM)
     vmem = pl.BlockSpec(memory_space=pltpu.VMEM)
     V = pltpu.VMEM
     dma = pltpu.SemaphoreType.DMA
@@ -281,7 +287,7 @@
             jax.ShapeDtypeStruct((n_dp * rows, lat), BF16),
             jax.ShapeDtypeStruct((n_dp * rows, lat), BF16),
         ),
-        in_specs=[any_] * 7 + [vmem] * 2,
+        in_specs=[hbm] * 9,
         out_specs=(vmem, any_, any_, any_, any_),
         scratch_shapes=[
             V((rows, width), BF16), V((rows, width), BF16),
@@ -291,13 +297,13 @@
             *[V((slots, lat), BF16)] * 8,
             V((slots, hidden), F32), V((slots, hidden), F32),
             V((slots, hidden), BF16), V((slots, hidden), BF16), V((slots, hidden), BF16),
-            V((rows, lat), BF16), V((rows, lat), BF16),
-            dma((7,)), dma((4,)), dma((4, n_e)), dma((4, n_e)),
+            V((rows, lat), BF16), V((rows, lat), BF16), V((top, rows), F32), V((top, rows), jnp.int32),
+            dma((9,)), dma((4,)), dma((4, n_e)), dma((4, n_e)),
             dma((2, n_dp)), dma((2, n_dp)),
             dma((n_dp,)), dma((n_dp,)), dma((n_dp,)), dma((n_dp,)), dma((4,)),
         ],
         compiler_params=pltpu.CompilerParams(
-            collective_id=0, has_side_effects=True, vmem_limit_bytes=48 * 1024 * 1024
+            collective_id=0, has_side_effects=True, vmem_limit_bytes=56 * 1024 * 1024
         ),
     )(tokens, out_grad, w_in, w_out, w_gate, w_up, w_down, gate_logits.T, expert_ids.T)
     token_grad, grad_in, grad_out, logit_grad = pl.pallas_call(
@@ -317,7 +323,7 @@
             V((rows, width), BF16), V((dw, lat), F32), V((lat, dw), F32),
             dma((5,)), dma((3,)),
         ],
-        compiler_params=pltpu.CompilerParams(vmem_limit_bytes=24 * 1024 * 1024),
+        compiler_params=pltpu.CompilerParams(vmem_limit_bytes=58 * 1024 * 1024),
     )(w_in, *arrays[1:], arrays[0])
     return token_grad, logit_grad.T, grad_in, grad_out
 

time: 59.2 us -> 55.4 us (0.936)
  local copies, waits for them, and re-layouts: 5.88 us -> 0 us
  Pallas kernels: 52.3 us -> 54.6 us
    unnamed x14 -> x0, local copies, waits for them, and re-layouts: 5.88 us -> none
    pallas_call x1, Pallas kernels: 3.47 us -> 5.16 us  [body(): pl.pallas_call(functools.partial(last_kernel, n_dp), out_shape=(jax.Shape...]
    pallas_call x1, Pallas kernels: 48.8 us -> 49.5 us  [body(): pl.pallas_call(functools.partial(kernel, n_e, n_dp, cap), out_shape=(jax....]
where the time goes in v3:
time: 55.4 us; the launch traced here: 55.3 us
  Pallas kernels  54.6 us (99%)
  between operations  0.64 us (1%)
    pallas_call x1, Pallas kernels, body(): pl.pallas_call(functools.partial(kernel, n_e, n_dp, cap), out_shape=(jax....  49.5 us
    pallas_call x1, Pallas kernels, body(): pl.pallas_call(functools.partial(last_kernel, n_dp), out_shape=(jax.Shape...  5.16 us

profile of v3, /device:TPU:0, one launch (start us, length us, event | category | flops | bytes accessed | tf_op | source)
XLA Modules:
  0.0 55.3 jit_solution(11693318866041917173)
XLA Ops:
  0.6 49.5 %shard_map.120 = (f32[2,128]{1,0:T(2,128)}, bf16[512,512]{1,0:T(8,128)(2,1)}, bf16[512,512]{1,0:T(8,128)(2,1)}, bf16[512,512]{1,0:T(8,128)(2,1)}, bf16[512,512]{1,0:T(8,128)(2,1)}) custom-call(bf16[128,2048]{1,0:T(8,128)(2,1)} %tokens_h.1, bf16[128,2048]{1,0:T(8,128)(2,1)} %dy_h.1, bf16[2048,512]{1,0:T(8,128)(2,1)} %w_in_h.3, bf16[512,2048]{1,0:T(8,128)(2,1)} %w_out_h.1, ...), custom_call_target="tpu_custom_call" | custom-call | tf_op jit(solution)/shard_map/pallas_call | solution.py:281
  50.1 5.2 %shard_map.121 = (bf16[128,2048]{1,0:T(8,128)(2,1)}, f32[1,512,512]{2,1,0:T(8,128)}, f32[1,512,512]{2,1,0:T(8,128)}, f32[2,128]{1,0:T(2,128)}) custom-call(bf16[2048,512]{1,0:T(8,128)(2,1)} %w_in_h.3, bf16[512,512]{1,0:T(8,128)(2,1)} %get-tuple-element.13.tok_h, bf16[512,512]{1,0:T(8,128)(2,1)} %get-tuple-element.14.dy_h, ...), custom_call_target="tpu_custom_call" | custom-call | tf_op jit(solution)/shard_map/pallas_call | solution.py:309
